TPU v7x, 256 devices: a whole 4x4x8 slice. The times are simulated.
256 devices in a mesh: row: 8 (over x, core), col: 32 (over z, y).
Axes of the slice: x: 4, y: 4, z: 8, core: 2. Of those that a mesh axis runs over, the one named last changes fastest.
Arguments:
- matrix: bfloat16 [12, 2048, 3, 8192], P(None, 'row', None, 'col'), may hold values from -5 to 101, as said below
Outputs:
- factored: bfloat16 [12, 2048, 3, 8192], P(None, 'row', None, 'col')
Inputs may be any that keep to these rules, and one draw needn't show every extreme that they name: `matrix`: each diagonal entry is a value between 4 * sqrt(256) and 6 * sqrt(256) plus an entry of order one; every other entry is of order one.
All inputs are finite; a program needn't handle non-finite values.
Results may differ from a plain program's by a relative error of at most 0.0052.
Values may be sent and summed in bfloat16 or wider, within the bound.
A program may use at most 64 MiB of HBM per device.

v0:
```python
import jax
import jax.numpy as jnp
from jax import lax
from jax.sharding import PartitionSpec as P

STEPS = 2


def broadcast(block, axis, owner):
    block = jnp.where(lax.axis_index(axis) == owner, block, jnp.zeros_like(block))
    return lax.psum(block, axis)


def factor_panel(panel):
    height, breadth = panel.shape
    ridx = jnp.arange(height)
    cidx = jnp.arange(breadth)

    def turn(j, work):
        pivot = lax.dynamic_slice(work, (j, j), (1, 1))[0, 0]
        column = lax.dynamic_slice_in_dim(work, j, 1, 1)[:, 0]
        row_vals = lax.dynamic_slice_in_dim(work, j, 1, 0)[0]
        lcol = jnp.where(ridx > j, column / pivot, jnp.zeros_like(column))
        urow = jnp.where(cidx > j, row_vals, jnp.zeros_like(row_vals))
        work = work - lcol[:, None] * urow[None, :]
        return jnp.where((ridx > j)[:, None] & (cidx == j)[None, :], lcol[:, None], work)

    return lax.fori_loop(0, breadth, turn, panel)


def factor_block(block):
    size = block.shape[0]
    width_sub = min(32, size)
    work = block
    for first in range(0, size, width_sub):
        last = first + width_sub
        panel = factor_panel(work[first:, first:last])
        work = work.at[first:, first:last].set(panel)
        if last < size:
            unit_lower = jnp.tril(panel[:width_sub], -1) + jnp.eye(width_sub, dtype=work.dtype)
            right_rows = jax.scipy.linalg.solve_triangular(
                unit_lower, work[first:last, last:], lower=True, unit_diagonal=True
            )
            work = work.at[first:last, last:].set(right_rows)
            trailing = jnp.dot(panel[width_sub:], right_rows, precision=lax.Precision.HIGHEST)
            work = work.at[last:, last:].add(-trailing)
    return work


def series_inverse(strict):
    size = strict.shape[0]
    eye = jnp.eye(size, dtype=strict.dtype)
    term = -strict
    result = eye + term
    for level in range((size - 1).bit_length() - 1):
        term = jnp.dot(term, term, precision=lax.Precision.HIGHEST)
        result = jnp.dot(result, eye + term, precision=lax.Precision.HIGHEST)
    return result


def invert_factors(packed):
    diag_vals = jnp.diagonal(packed)
    linv = series_inverse(jnp.tril(packed, -1))
    scaled = jnp.triu(packed, 1) / diag_vals[:, None]
    uinv = series_inverse(scaled) / diag_vals[None, :]
    return (linv.astype(jnp.bfloat16), uinv.astype(jnp.bfloat16))


def on_device(matrix):
    brows, width, bcols = (matrix.shape[0], matrix.shape[1], matrix.shape[2])
    nrow = lax.axis_size("row")
    ncol = lax.axis_size("col")
    my_row = lax.axis_index("row")
    my_col = lax.axis_index("col")
    row_ids = jnp.arange(brows) * nrow + my_row
    col_ids = jnp.arange(bcols) * ncol + my_col
    current = matrix
    for k in range(STEPS):
        owner_row = k % nrow
        owner_col = k % ncol
        local_r = k // nrow
        local_c = k // ncol
        below = row_ids > k
        right = col_ids > k
        col_panel = current[:, :, local_c, :]
        diag_block = broadcast(current[local_r, :, local_c, :], "row", owner_row)
        packed = factor_block(diag_block.astype(jnp.float32))
        linv, uinv = invert_factors(packed)
        lower = jnp.dot(
            col_panel.reshape(brows * width, width), uinv, preferred_element_type=jnp.float32
        )
        lower = lower.astype(jnp.bfloat16).reshape(brows, width, width)
        lower = jnp.where(below[:, None, None], lower, jnp.zeros_like(lower))
        lpanel, linv_recv = (broadcast(lower, "col", owner_col), broadcast(linv, "col", owner_col))
        row_panel = current[local_r].reshape(width, bcols * width)
        upper = jnp.dot(linv_recv, row_panel, preferred_element_type=jnp.float32)
        upper = upper.astype(jnp.bfloat16).reshape(width, bcols, width)
        upper = jnp.where(right[None, :, None], upper, jnp.zeros_like(upper))
        upanel = broadcast(upper, "row", owner_row)
        left_rows = lpanel.reshape(brows * width, width)
        change = jnp.dot(
            left_rows, upanel.reshape(width, bcols * width), preferred_element_type=jnp.float32
        )
        change = change.reshape(brows, width, bcols, width)
        updated = (current.astype(jnp.float32) - change).astype(jnp.bfloat16)
        is_pcol = my_col == owner_col
        is_prow = my_row == owner_row
        new_col = jnp.where(below[:, None, None], lpanel, col_panel)
        diag_here = jnp.where(is_prow, packed.astype(jnp.bfloat16), new_col[local_r])
        new_col = new_col.at[local_r].set(diag_here)
        updated = updated.at[:, :, local_c, :].set(
            jnp.where(is_pcol, new_col, updated[:, :, local_c, :])
        )
        old_row = updated[local_r]
        new_row = jnp.where(right[None, :, None], upanel, old_row)
        updated = updated.at[local_r].set(jnp.where(is_prow, new_row, old_row))
        current = updated
    return current


def solution(mesh):
    placed = (P(None, "row", None, "col"),)
    return jax.shard_map(
        on_device,
        mesh=mesh,
        in_specs=placed,
        out_specs=P(None, "row", None, "col"),
        check_vma=False,
    )
```

profile of v0, /device:TPU:36, one launch (start us, length us, event | category | flops | bytes accessed | tf_op | source)
XLA Modules:
  0.0 1495.3 jit_solution(3878975245424805657)
XLA Ops:
  10.3 62.5 %all-reduce.9.cloned.1.call-done = bf16[256,256]{1,0:T(8,128)(2,1)} async-done(((bf16[256,256]{1,0:T(8,128)(2,1)}), bf16[256,256]{1,0:T(8,128)(2,1)}) %all-reduce.9.cloned.1.call-update) | async-done | bytes 131088 | tf_op jit(solution)/shard_map/psum | solution.py:11
  73.8 47.3 %while.292 = (s32[]{:T(128)}, f32[256,32]{0,1:T(8,128)S(1)}, s32[]{:T(128)}) while((s32[]{:T(128)}, f32[256,32]{0,1:T(8,128)S(1)}, s32[]{:T(128)}) %tuple.716), condition=%wide.region_3.4_spmd.clone.clone, body=%wide.region_2.3_spmd.clone.clone.sunk | while | flops 33634 | bytes 136465 | solution.py:28
  133.0 47.3 %while.293 = (s32[]{:T(128)}, f32[224,32]{0,1:T(8,128)S(1)}, s32[]{:T(128)}) while((s32[]{:T(128)}, f32[224,32]{0,1:T(8,128)S(1)}, s32[]{:T(128)}) %tuple.719), condition=%wide.region_6.8_spmd.clone.clone, body=%wide.region_5.7_spmd.clone.clone.sunk | while | flops 29442 | bytes 119601 | solution.py:28
  189.2 47.3 %while.294 = (s32[]{:T(128)}, f32[192,32]{0,1:T(8,128)S(1)}, s32[]{:T(128)}) while((s32[]{:T(128)}, f32[192,32]{0,1:T(8,128)S(1)}, s32[]{:T(128)}) %tuple.722), condition=%wide.region_8.11_spmd.clone.clone, body=%wide.region_7.10_spmd.clone.clone.sunk | while | flops 25250 | bytes 102737 | solution.py:28
  244.9 47.3 %while.295 = (s32[]{:T(128)}, f32[160,32]{0,1:T(8,128)S(1)}, s32[]{:T(128)}) while((s32[]{:T(128)}, f32[160,32]{0,1:T(8,128)S(1)}, s32[]{:T(128)}) %tuple.725), condition=%wide.region_10.14_spmd.clone.clone, body=%wide.region_9.13_spmd.clone.clone.sunk | while | flops 21058 | bytes 85873 | solution.py:28
  297.2 47.3 %while.296 = (s32[]{:T(128)}, f32[128,32]{0,1:T(8,128)S(1)}, s32[]{:T(128)}) while((s32[]{:T(128)}, f32[128,32]{0,1:T(8,128)S(1)}, s32[]{:T(128)}) %tuple.728), condition=%wide.region_12.17_spmd.clone.clone, body=%wide.region_11.16_spmd.clone.clone.sunk | while | flops 16994 | bytes 69901 | solution.py:28
  350.6 47.0 %while.297 = (s32[]{:T(128)}, f32[96,32]{0,1:T(8,128)S(1)}, s32[]{:T(128)}) while((s32[]{:T(128)}, f32[96,32]{0,1:T(8,128)S(1)}, s32[]{:T(128)}) %tuple.731), condition=%wide.region_14.20_spmd.clone.clone, body=%wide.region_13.19_spmd.clone.clone.sunk | while | flops 12770 | bytes 53069 | solution.py:28
  403.9 46.5 %while.298 = (s32[]{:T(128)}, f32[64,32]{0,1:T(8,128)S(1)}, s32[]{:T(128)}) while((s32[]{:T(128)}, f32[64,32]{0,1:T(8,128)S(1)}, s32[]{:T(128)}) %tuple.734), condition=%wide.region_16.23_spmd.clone.clone, body=%wide.region_15.22_spmd.clone.clone.sunk | while | flops 8546 | bytes 36237 | solution.py:28
  456.5 45.8 %while.299 = (s32[]{:T(128)}, f32[32,32]{0,1:T(8,128)S(1)}, s32[]{:T(128)}) while((s32[]{:T(128)}, f32[32,32]{0,1:T(8,128)S(1)}, s32[]{:T(128)}) %tuple.737), condition=%wide.region_18.26_spmd.clone.clone, body=%wide.region_17.25_spmd.clone.clone.sunk | while | flops 4322 | bytes 19401 | solution.py:28
  524.4 153.9 %all-reduce.19.cloned.1.call-done = (bf16[12,256,256]{2,1,0:T(8,128)(2,1)}, bf16[256,256]{1,0:T(8,128)(2,1)}) async-done(((bf16[12,256,256]{2,1,0:T(8,128)(2,1)}, bf16[256,256]{1,0:T(8,128)(2,1)}), (bf16[12,256,256]{2,1,0:T(8,128)(2,1)}, bf16[256,256]{1,0:T(8,128)(2,1)})) %all-reduce.19.cloned.1.call-update) | async-done | bytes 1703952 | tf_op jit(solution)/shard_map/psum | solution.py:11
  682.9 57.8 %all-reduce.11.cloned.1.call-done = bf16[256,3,256]{2,0,1:T(8,128)(2,1)} async-done(((bf16[256,3,256]{2,0,1:T(8,128)(2,1)}), bf16[256,3,256]{2,0,1:T(8,128)(2,1)}) %all-reduce.11.cloned.1.call-update) | async-done | bytes 393232 | tf_op jit(solution)/shard_map/psum | solution.py:11
  742.6 4.0 subtract_convert_fusion.1
  752.7 61.4 %all-reduce.13.cloned.1.call-done = bf16[256,256]{1,0:T(8,128)(2,1)} async-done(((bf16[256,256]{1,0:T(8,128)(2,1)}), bf16[256,256]{1,0:T(8,128)(2,1)}) %all-reduce.13.cloned.1.call-update) | async-done | bytes 131088 | tf_op jit(solution)/shard_map/psum | solution.py:11
  815.1 48.4 %while.300 = (s32[]{:T(128)}, f32[256,32]{0,1:T(8,128)S(1)}, s32[]{:T(128)}) while((s32[]{:T(128)}, f32[256,32]{0,1:T(8,128)S(1)}, s32[]{:T(128)}) %tuple.740), condition=%wide.region_24.32_spmd.clone.clone, body=%wide.region_23.31_spmd.clone.clone.sunk | while | flops 33634 | bytes 136465 | solution.py:28
  875.4 47.7 %while.301 = (s32[]{:T(128)}, f32[224,32]{0,1:T(8,128)S(1)}, s32[]{:T(128)}) while((s32[]{:T(128)}, f32[224,32]{0,1:T(8,128)S(1)}, s32[]{:T(128)}) %tuple.743), condition=%wide.region_26.34_spmd.clone.clone, body=%wide.region_25.33_spmd.clone.clone.sunk | while | flops 29442 | bytes 119601 | solution.py:28
  932.0 47.7 %while.302 = (s32[]{:T(128)}, f32[192,32]{0,1:T(8,128)S(1)}, s32[]{:T(128)}) while((s32[]{:T(128)}, f32[192,32]{0,1:T(8,128)S(1)}, s32[]{:T(128)}) %tuple.746), condition=%wide.region_28.36_spmd.clone.clone, body=%wide.region_27.35_spmd.clone.clone.sunk | while | flops 25250 | bytes 102737 | solution.py:28
  988.0 47.7 %while.303 = (s32[]{:T(128)}, f32[160,32]{0,1:T(8,128)S(1)}, s32[]{:T(128)}) while((s32[]{:T(128)}, f32[160,32]{0,1:T(8,128)S(1)}, s32[]{:T(128)}) %tuple.749), condition=%wide.region_30.38_spmd.clone.clone, body=%wide.region_29.37_spmd.clone.clone.sunk | while | flops 21058 | bytes 85873 | solution.py:28
  1040.7 47.7 %while.304 = (s32[]{:T(128)}, f32[128,32]{0,1:T(8,128)S(1)}, s32[]{:T(128)}) while((s32[]{:T(128)}, f32[128,32]{0,1:T(8,128)S(1)}, s32[]{:T(128)}) %tuple.752), condition=%wide.region_32.40_spmd.clone.clone, body=%wide.region_31.39_spmd.clone.clone.sunk | while | flops 16994 | bytes 69901 | solution.py:28
  1094.6 47.4 %while.305 = (s32[]{:T(128)}, f32[96,32]{0,1:T(8,128)S(1)}, s32[]{:T(128)}) while((s32[]{:T(128)}, f32[96,32]{0,1:T(8,128)S(1)}, s32[]{:T(128)}) %tuple.755), condition=%wide.region_34.42_spmd.clone.clone, body=%wide.region_33.41_spmd.clone.clone.sunk | while | flops 12770 | bytes 53069 | solution.py:28
  1148.3 46.9 %while.306 = (s32[]{:T(128)}, f32[64,32]{0,1:T(8,128)S(1)}, s32[]{:T(128)}) while((s32[]{:T(128)}, f32[64,32]{0,1:T(8,128)S(1)}, s32[]{:T(128)}) %tuple.758), condition=%wide.region_36.44_spmd.clone.clone, body=%wide.region_35.43_spmd.clone.clone.sunk | while | flops 8546 | bytes 36237 | solution.py:28
  1201.3 43.0 %while.307 = (s32[]{:T(128)}, f32[32,32]{0,1:T(8,128)S(1)}, s32[]{:T(128)}) while((s32[]{:T(128)}, f32[32,32]{0,1:T(8,128)S(1)}, s32[]{:T(128)}) %tuple.761), condition=%wide.region_38.46_spmd.clone.clone, body=%wide.region_37.45_spmd.clone.clone.sunk | while | flops 4322 | bytes 19401 | solution.py:28
  1262.0 153.8 %all-reduce.17.cloned.1.call-done = (bf16[12,256,256]{2,1,0:T(8,128)(2,1)}, bf16[256,256]{1,0:T(8,128)(2,1)}) async-done(((bf16[12,256,256]{2,1,0:T(8,128)(2,1)}, bf16[256,256]{1,0:T(8,128)(2,1)}), (bf16[12,256,256]{2,1,0:T(8,128)(2,1)}, bf16[256,256]{1,0:T(8,128)(2,1)})) %all-reduce.17.cloned.1.call-update) | async-done | bytes 1703952 | tf_op jit(solution)/shard_map/psum | solution.py:11
  1420.1 58.1 %all-reduce.15.cloned.1.call-done = bf16[256,3,256]{2,0,1:T(8,128)(2,1)} async-done(((bf16[256,3,256]{2,0,1:T(8,128)(2,1)}), bf16[256,3,256]{2,0,1:T(8,128)(2,1)}) %all-reduce.15.cloned.1.call-update) | async-done | bytes 393232 | tf_op jit(solution)/shard_map/psum | solution.py:11
  1480.1 4.0 subtract_convert_fusion
  (3796 shorter events, 909.2 us)
Async XLA Ops:
  6.5 66.2 %all-reduce.9.cloned.1.call-start = ((), (), s32[]{:S(2)}) async-start(), calls=%async_computation | async-start | bytes 262144 | tf_op jit(solution)/shard_map/psum | solution.py:11
  8.1 670.1 %all-reduce.19.cloned.1.call-start = ((), (), s32[]{:S(2)}) async-start(), calls=%async_computation.5 | async-start | bytes 3407872 | tf_op jit(solution)/shard_map/psum | solution.py:11
  8.2 0.7 copy-start.7
  8.2 1.9 slice-start
  72.8 48.4 %copy-start.5 = (bf16[256,256]{1,0:T(8,128)(2,1)S(1)}, bf16[256,256]{1,0:T(8,128)(2,1)}, u32[]{:S(2)}) copy-start(bf16[256,256]{1,0:T(8,128)(2,1)} %all-reduce.9.cloned.1.call-done) | copy-start | bytes 393220
  523.0 1.1 slice-start.1
  524.1 216.7 %all-reduce.11.cloned.1.call-start = ((), (), s32[]{:S(2)}) async-start(), calls=%async_computation.1 | async-start | bytes 786432 | tf_op jit(solution)/shard_map/psum | solution.py:11
  679.5 1.4 copy-start.2
  680.7 133.4 %all-reduce.13.cloned.1.call-start = ((), (), s32[]{:S(2)}) async-start(), calls=%async_computation.2 | async-start | bytes 262144 | tf_op jit(solution)/shard_map/psum | solution.py:11
  746.6 2.9 copy-start.3
  747.4 2.2 copy-start
  750.4 665.4 %all-reduce.17.cloned.1.call-start = ((), (), s32[]{:S(2)}) async-start(), calls=%async_computation.4 | async-start | bytes 3407872 | tf_op jit(solution)/shard_map/psum | solution.py:11
  814.1 49.6 %copy-start.6 = (bf16[256,256]{1,0:T(8,128)(2,1)S(1)}, bf16[256,256]{1,0:T(8,128)(2,1)}, u32[]{:S(2)}) copy-start(bf16[256,256]{1,0:T(8,128)(2,1)} %all-reduce.13.cloned.1.call-done) | copy-start | bytes 393220
  1261.5 216.7 %all-reduce.15.cloned.1.call-start = ((), (), s32[]{:S(2)}) async-start(), calls=%async_computation.3 | async-start | bytes 786432 | tf_op jit(solution)/shard_map/psum | solution.py:11
  1417.0 1.4 copy-start.1
  1484.1 1.0 copy-start.4
Sparse Core Ops, SparseCore 0:
  9.7 63.0 all-reduce.8
  524.2 154.0 all-reduce.18
  680.8 59.8 all-reduce.10
  750.5 63.5 all-reduce.12
  1261.6 154.0 all-reduce.16
  1418.3 59.8 all-reduce.14
where the time goes:
time: 1510 us; the launch traced here: 1500 us
  waiting for transfers between devices  547 us (36%)
  local copies, waits for them, and re-layouts  436 us (29%)
  other arithmetic  430 us (28%)
  matrix products  51.1 us (3%)
  loops' own time  15.4 us (1%)
  between operations  15.3 us (1%)
    psum x6, waiting for transfers between devices, broadcast(): return lax.psum(block, axis)  547 us
    dynamic_slice x512, local copies, waits for them, and re-layouts, turn(): pivot = lax.dynamic_slice(work, (j, j), (1, 1))[0, 0]  309 us
    select_n x256, other arithmetic, turn(): lcol = jnp.where(ridx > j, column / pivot, jnp.zeros_like(column))  165 us
    broadcast_in_dim x256, other arithmetic, turn(): jnp.where((ridx > j)[:, None] & (cidx == j)[None, :], lcol[:, None], work)  164 us
    while x512, local copies, waits for them, and re-layouts  47.8 us
    select_n x512, other arithmetic, turn(): jnp.where((ridx > j)[:, None] & (cidx == j)[None, :], lcol[:, None], work)  39.5 us
    another operation x29, other arithmetic, factor_block(): jax.scipy.linalg.solve_triangular(unit_lower, work[first:last, last:], lo...  35.2 us
  transfers between devices with their start and end apart: 6, of which 6 were waited for; matrix products, arithmetic and copies ran while one was open for 1% of the time, Pallas kernels for 0%

commit v1 on v0

v1 whole, which is shorter than its diff:
```python
import functools

import jax
import jax.experimental.pallas as pl
import jax.experimental.pallas.tpu as pltpu
import jax.numpy as jnp
from jax import lax
from jax.sharding import PartitionSpec as P

NB = 256
B = 64
BR, BC = 12, 3
N_ROW, N_COL, N_Y, N_Z = 8, 32, 4, 8
F32, BF = jnp.float32, jnp.bfloat16
MESH = pl.DeviceIdType.MESH
CHUNKS = 2 * BR


def recip(p):
    r = pl.reciprocal(p, approx=True)
    return r * (2.0 - p * r)

def bcast_lane(t, n):
    return jnp.broadcast_to(t[:, n:n + 1], (8, 128))

def bcast_row(t, j):
    return jnp.broadcast_to(t[j:j + 1, :], (8, 128))

def base(m1, m2, tick):
    sub = lax.broadcasted_iota(jnp.int32, (8, 128), 0)
    for k in range(8):
        tick(k)
        n = range(k, 8)
        v = {i: [bcast_lane(m1[i], 8 * k + j) for j in range(8)] for i in n}
        w = {i: [bcast_lane(m2[i], 8 * k + j) for j in range(8)] for i in n}
        scale = jnp.ones((8, 128), F32)
        for j in range(8):
            r = recip(bcast_row(v[k][j], j))
            scale = jnp.where(sub == j, r, scale)
            lv = {i: v[i][j] * r for i in n}
            lw = {i: w[i][j] * r for i in n}
            lv[k] = jnp.where(sub > j, lv[k], 0.0)
            lw[k] = jnp.where(sub > j, lw[k], 0.0)
            for t in range(j + 1, 8):
                a, b = bcast_row(v[k][t], j), bcast_row(w[k][t], j)
                for i in n:
                    v[i][t] = v[i][t] - lv[i] * a
                    w[i][t] = w[i][t] - lw[i] * b
            a, b = bcast_row(m1[k], j), bcast_row(m2[k], j)
            for i in n:
                m1[i] = m1[i] - lv[i] * a
                m2[i] = m2[i] - lw[i] * b
        m2[k] = m2[k] * scale
    return jnp.concatenate(m1, 0), jnp.concatenate(m2, 0)

def split(a):
    h = a.astype(BF)
    return h, (a - h.astype(F32)).astype(BF)

def dot3(a, b, nt=False):
    d = functools.partial(lax.dot_general, dimension_numbers=(((1,), (1 if nt else 0,)), ((), ())), preferred_element_type=F32)
    return d(a[0], b[0]) + (d(a[0], b[1]) + d(a[1], b[0]))

def block_step(q, a1, a2, tick):
    rows = pl.ds(pl.multiple_of(q * B, B), B)
    odd = lax.rem(q, 2) == 1
    half = lax.div(q, 2)
    lane = lax.broadcasted_iota(jnp.int32, (B, 128), 1)
    sub = lax.broadcasted_iota(jnp.int32, (B, 128), 0)
    eye = (lane - B == sub).astype(F32)
    def diag(a):
        x = a[half, rows, :]
        x = jnp.where(odd, pltpu.roll(x, B, 1), x)
        x = jnp.where(lane < B, x, eye)
        return [x[8 * i:8 * i + 8] for i in range(8)]
    m1, m2 = base(diag(a1), diag(a2), tick)
    r1, r2 = pltpu.roll(m1, B, 1), pltpu.roll(m2, B, 1)
    mine = (lane >= B) == odd
    li, ui = r1[:, :B], r2[:, :B]
    lip = split(jnp.where(mine, jnp.where(odd, m1, r1), 0.0))
    uip = split(jnp.where(mine, jnp.where(odd, m2, r2), 0.0))
    below = lax.broadcasted_iota(jnp.int32, (256, B), 0) >= (q + 1) * B
    l21 = split(jnp.where(below, dot3(split(a1[half]), uip, True), 0.0))
    u12 = split(jnp.where(below, dot3(split(a2[half]), lip, True), 0.0))
    for a, li_, mult, m, r in ((a1, split(li), l21, m1, r1), (a2, split(ui), u12, m2, r2)):
        old = a[:, rows, :]
        p = dot3(li_, split(jnp.concatenate([old[i] for i in range(4)], 1)))
        prod = dot3(mult, split(p))
        for i in range(4):
            a[i] = a[i] - prod[:, 128 * i:128 * i + 128]
            a[i, rows, :] = p[:, 128 * i:128 * i + 128]
        a[half, rows, :] = jnp.where(mine, jnp.where(odd, r, m), a[half, rows, :])

def load(a, a1, a2):
    eye = (lax.broadcasted_iota(jnp.int32, (256, 256), 0) == lax.broadcasted_iota(jnp.int32, (256, 256), 1)).astype(F32)
    for ref, x in ((a1, a), (a2, jnp.transpose(a))):
        for i in range(2):
            ref[i] = x[:, 128 * i:128 * i + 128]
            ref[2 + i] = eye[:, 128 * i:128 * i + 128]

def full(a, i):
    return jnp.concatenate([a[i], a[i + 1]], 1)

def results(a1, a2):
    ri = lax.broadcasted_iota(jnp.int32, (256, 256), 0); ci = lax.broadcasted_iota(jnp.int32, (256, 256), 1)
    packed = jnp.where(ri <= ci, full(a1, 0), jnp.transpose(full(a2, 0)))
    return packed, full(a1, 2), jnp.transpose(full(a2, 2))


def nn(a, b):
    return jnp.dot(a, b, preferred_element_type=F32)


def gather_factor(
    a, col_out, row_out, packed, linv, uinv, l10_out, u01_out,
    col, row, pieces, a1, a2,
    s1_send, s2_send, s3_send, p_recv, s3_recv,
    col_send, col_recv, row_send, row_recv, local_sem,
):
    r, c = lax.axis_index("row"), lax.axis_index("col")
    z, y = lax.div(c, N_Y), lax.rem(c, N_Y)
    core = lax.rem(r, 2)

    def send(src, dst, ssem, rsem, dev):
        return pltpu.make_async_remote_copy(
            src_ref=src, dst_ref=dst, send_sem=ssem, recv_sem=rsem, device_id=dev, device_id_type=MESH
        )

    barrier = pltpu.get_barrier_semaphore()

    @pl.loop(1, N_COL)
    def _(i):
        pl.semaphore_signal(barrier, inc=1, device_id=(r, lax.rem(c + i, N_COL)), device_id_type=MESH)

    @pl.loop(1, N_ROW)
    def _(i):
        pl.semaphore_signal(barrier, inc=1, device_id=(lax.rem(r + i, N_ROW), c), device_id_type=MESH)

    pl.semaphore_wait(barrier, N_COL - 1 + N_ROW - 1)

    def diag_piece(p):
        return a.at[0, 0, lax.div(p, 16), pl.ds(pl.multiple_of(lax.rem(lax.div(p, 2), 8) * 16, 16), 16),
                    pl.ds(pl.multiple_of(lax.rem(p, 2) * 128, 128), 128)]

    def own_copy(b):
        return pltpu.make_async_copy(diag_piece(c), pieces.at[b, c], p_recv.at[b])

    for b in range(4):
        @pl.when((r == b // 2) & (c == b % 2))
        def _(b=b):
            @pl.loop(1, N_COL)
            def _(i):
                dst = lax.rem(c + i, N_COL)
                send(diag_piece(dst), pieces.at[b, dst], s1_send.at[0], p_recv.at[b], (r, dst)).start()

            own_copy(b).start()

    dist_z = jnp.minimum(z, N_Z - z)
    dist_y = [lax.rem(y - b + N_Y, N_Y) for b in range(2)]
    source = [(z == 0) & (dist_y[b] == 0) for b in range(2)]

    def load_panel(b):
        return pltpu.make_async_copy(a.at[:, 0], col.at[b], local_sem.at[0])

    def load_row():
        return pltpu.make_async_copy(a.at[0], row.at[core], local_sem.at[1])

    for b in range(2):
        @pl.when(source[b])
        def _(b=b):
            load_panel(b).start()

    @pl.when(r < 2)
    def _():
        load_row().start()

    def arrived(b):
        own = (r == b // 2) & (c == b % 2)

        @pl.when(own)
        def _():
            own_copy(b).wait()

        @pl.when(jnp.logical_not(own))
        def _():
            send(pieces.at[b, c], pieces.at[b, c], s1_send.at[0], p_recv.at[b], (r, c)).wait_recv()

    def to_rows(b):
        for i in range(1, N_ROW):
            dst = lax.rem(r + i, N_ROW)
            yield send(pieces.at[b, c], pieces.at[b, c], s2_send.at[b % 2, i - 1], p_recv.at[b], (dst, c))

    def spread_rows(blocks):
        for b in blocks:
            @pl.when(r == b // 2)
            def _(b=b):
                arrived(b)
                for copy in to_rows(b):
                    copy.start()

    def to_cols(kind, dst):
        block = pieces.at[pl.ds(kind, 1 + 2 * kind), c]
        return send(block, block, s3_send.at[kind], s3_recv.at[kind], (r, dst))

    def spread_cols(kind, blocks):
        for b in blocks:
            @pl.when(r != b // 2)
            def _(b=b):
                arrived(b)

        @pl.loop(1, N_COL)
        def _(i):
            to_cols(kind, lax.rem(c + i, N_COL)).start()

    def all_pieces(kind):
        block = pieces.at[pl.ds(kind, 1 + 2 * kind), pl.ds(0, N_COL - 1)]
        return send(block, block, s3_send.at[kind], s3_recv.at[kind], (r, c))

    spread_rows((0,))
    spread_cols(0, (0,))
    for b in range(2):
        @pl.when(source[b])
        def _(b=b):
            load_panel(b).wait()

    @pl.when(r < 2)
    def _():
        load_row().wait()

    def forwards(b, half):
        z_up = (dist_y[b] == 0) & (z <= 3)
        z_down = (dist_y[b] == 0) & ((z == 0) | (z >= 6))
        if half == 0:
            y_on, y_dst = dist_y[b] <= 2, lax.rem(y + 1, N_Y)
        else:
            y_on, y_dst = dist_y[b] != 1, lax.rem(y + N_Y - 1, N_Y)
        z_dst = lambda dz: lax.rem(z + dz + N_Z, N_Z) * N_Y + y
        return ((z_up, z_dst(1)), (z_down, z_dst(-1)), (y_on, z * N_Y + y_dst))

    def chunk_copy(b, half, i, way, dst):
        block = col.at[b, i, half]
        return send(block, block, col_send.at[b, half, i, way], col_recv.at[b, half, i], (r, dst))

    def relay(slot):
        for b in range(2):
            for half in range(2):
                dist = dist_z + (dist_y[b] if half == 0 else lax.rem(N_Y - dist_y[b], N_Y))
                m = slot - dist - (2 * half + b)
                i = lax.div(m, 4)

                @pl.when((m >= 0) & (lax.rem(m, 4) == 0) & (i < BR))
                def _(b=b, half=half, i=i):
                    @pl.when(jnp.logical_not(source[b]))
                    def _():
                        chunk_copy(b, half, i, 0, c).wait_recv()

                    for way, (on, dst) in enumerate(forwards(b, half)):
                        @pl.when(on)
                        def _(way=way, dst=dst):
                            chunk_copy(b, half, i, way, dst).start()

    def row_copy(i, dst):
        block = row.at[core]
        return send(block, block, row_send.at[i], row_recv.at[core], (dst, c))

    def row_out_start():
        @pl.when(r < 2)
        def _():
            for i in range(1, 4):
                row_copy(i, r + 2 * i).start()

    def row_swap():
        @pl.when(r >= 2)
        def _():
            row_copy(0, r).wait_recv()

        row_copy(0, r + 1 - 2 * core).start()

    send(pieces.at[0, pl.ds(0, N_COL - 1)], pieces.at[0, pl.ds(0, N_COL - 1)],
         s3_send.at[0], s3_recv.at[0], (r, c)).wait_recv()

    def whole(b):
        x = pieces[b].astype(F32).reshape(16, 2, 16, 128)
        return jnp.concatenate([x[:, 0].reshape(NB, 128), x[:, 1].reshape(NB, 128)], 1)

    load(whole(0), a1, a2)

    @pl.loop(0, 8)
    def _(it):
        step = lax.div(it, 4)
        q = lax.rem(it, 4)

        @pl.when(it == 4)
        def _():
            all_pieces(1).wait_recv()
            l10 = nn(whole(2).astype(BF), uinv[0]).astype(BF)
            u01 = nn(linv[0], whole(1).astype(BF)).astype(BF)
            l10_out[...] = l10
            u01_out[...] = u01
            load((whole(3) - nn(l10, u01)).astype(BF).astype(F32), a1, a2)

        def tick(k):
            relay(it * 8 + k)
            if k == 1:
                @pl.when(it == 0)
                def _():
                    spread_rows((1, 2, 3))

            if k == 3:
                @pl.when(it == 0)
                def _():
                    spread_cols(1, (1, 2, 3))

            if k == 5:
                @pl.when(it == 0)
                def _():
                    row_out_start()

                @pl.when(it == 5)
                def _():
                    row_swap()

        block_step(q, a1, a2, tick)

        @pl.when(q == 3)
        def _():
            pk, li, ui = results(a1, a2)
            packed[step] = pk.astype(BF)
            linv[step] = li.astype(BF)
            uinv[step] = ui.astype(BF)

    out_copies = [
        pltpu.make_async_copy(col, col_out, local_sem.at[0]),
        pltpu.make_async_copy(row, row_out, local_sem.at[1]),
    ]
    out_copies[0].start()
    other = row.at[1 - core]
    send(other, other, row_send.at[0], row_recv.at[1 - core], (r, c)).wait_recv()
    out_copies[1].start()

    for b in range(4):
        @pl.when((r == b // 2) & (c == b % 2))
        def _(b=b):
            block = pieces.at[0, pl.ds(0, N_COL - 1)]
            send(block, block, s1_send.at[0], p_recv.at[b], (r, c)).wait_send()

        @pl.when(r == b // 2)
        def _(b=b):
            for copy in to_rows(b):
                copy.wait_send()

    for kind in range(2):
        all_pieces(kind).wait_send()

    @pl.when(r < 2)
    def _():
        for i in range(1, 4):
            row_copy(i, r).wait_send()

    row_copy(0, r).wait_send()

    for b in range(2):
        for half in range(2):
            for way, (on, dst) in enumerate(forwards(b, half)):
                @pl.when(on)
                def _(b=b, half=half, way=way, dst=dst):
                    @pl.loop(0, BR)
                    def _(i):
                        chunk_copy(b, half, i, way, dst).wait_send()

    for copy in out_copies:
        copy.wait()


def update(a, col, row, packed, linv, uinv, l10, u01, out, u):
    i = pl.program_id(0)
    r, c = lax.axis_index("row"), lax.axis_index("col")

    @pl.when(i == 0)
    def _():
        for j in range(BC):
            h = j * N_COL + c
            u0 = jnp.where(h > 0, nn(linv[0], row[0, j]), 0.0).astype(BF)
            r1 = (row[1, j].astype(F32) - nn(l10[...], u0)).astype(BF)
            u[0, j] = u0
            u[1, j] = jnp.where(h > 1, nn(linv[1], r1), 0.0).astype(BF)

    g = i * N_ROW + r
    l0 = jnp.where(g > 0, nn(col[0], uinv[0]), 0.0).astype(BF)
    c1 = (col[1].astype(F32) - nn(l0, u01[...])).astype(BF)
    l1 = jnp.where(g > 1, nn(c1, uinv[1]), 0.0).astype(BF)
    for j in range(BC):
        x = (a[j].astype(F32) - nn(l0, u[0, j])).astype(BF)
        out[j] = (x.astype(F32) - nn(l1, u[1, j])).astype(BF)

    @pl.when(c == 0)
    def _():
        out[0] = jnp.where(g > 0, l0, packed[0])

    @pl.when(c == 1)
    def _():
        out[0] = jnp.where(g > 1, l1, jnp.where(g == 1, packed[1], out[0]))

    @pl.when(i == 0)
    def _():
        for j in range(BC):
            h = j * N_COL + c
            out[j] = jnp.where((r == 0) & (h > 0), u[0, j], jnp.where((r == 1) & (h > 1), u[1, j], out[j]))


def on_device(matrix):
    a = matrix.transpose(0, 2, 1, 3)
    vmem = pl.BlockSpec(memory_space=pltpu.VMEM)
    hbm = pl.BlockSpec(memory_space=pl.ANY)
    shape = jax.ShapeDtypeStruct
    dma = pltpu.SemaphoreType.DMA
    col, row, packed, linv, uinv, l10, u01 = pl.pallas_call(
        gather_factor,
        out_shape=[
            shape((2, BR, 2, 128, NB), BF),
            shape((2, BC, 2, 128, NB), BF),
            shape((2, NB, NB), BF),
            shape((2, NB, NB), BF),
            shape((2, NB, NB), BF),
            shape((NB, NB), BF),
            shape((NB, NB), BF),
        ],
        in_specs=[hbm],
        out_specs=[hbm, hbm] + [vmem] * 5,
        scratch_shapes=[
            pltpu.VMEM((2, BR, 2, 128, NB), BF),
            pltpu.VMEM((2, BC, 2, 128, NB), BF),
            pltpu.VMEM((4, N_COL, 16, 128), BF),
            pltpu.VMEM((4, NB, 128), F32),
            pltpu.VMEM((4, NB, 128), F32),
            dma((1,)), dma((2, N_ROW - 1)), dma((2,)), dma((4,)), dma((2,)),
            dma((2, 2, BR, 3)), dma((2, 2, BR)), dma((4,)), dma((2,)), dma((2,)),
        ],
        compiler_params=pltpu.CompilerParams(
            collective_id=0, has_side_effects=True, vmem_limit_bytes=40 << 20
        ),
        name="gather_factor",
    )(a.reshape(BR, BC, 2, 128, NB))
    whole = lambda *dims: pl.BlockSpec(dims, lambda i: (0,) * len(dims))
    out = pl.pallas_call(
        update,
        grid=(BR,),
        out_shape=shape((BR, BC, NB, NB), BF),
        in_specs=[
            pl.BlockSpec((None, BC, NB, NB), lambda i: (i, 0, 0, 0)),
            pl.BlockSpec((2, None, NB, NB), lambda i: (0, i, 0, 0)),
            whole(2, BC, NB, NB),
            whole(2, NB, NB),
            whole(2, NB, NB),
            whole(2, NB, NB),
            whole(NB, NB),
            whole(NB, NB),
        ],
        out_specs=pl.BlockSpec((None, BC, NB, NB), lambda i: (i, 0, 0, 0)),
        scratch_shapes=[pltpu.VMEM((2, BC, NB, NB), BF)],
        compiler_params=pltpu.CompilerParams(vmem_limit_bytes=40 << 20),
        name="update",
    )(a, col.reshape(2, BR, NB, NB), row.reshape(2, BC, NB, NB), packed, linv, uinv, l10, u01)
    return out.transpose(0, 2, 1, 3)


def solution(mesh):
    placed = (P(None, "row", None, "col"),)
    return jax.shard_map(
        on_device,
        mesh=mesh,
        in_specs=placed,
        out_specs=P(None, "row", None, "col"),
        check_vma=False,
    )
```

time: 1510 us -> 216 us (0.14)
  the two profiles are of different devices: /device:TPU:36 before, /device:TPU:144 now
where the time goes in v1:
time: 216 us
  Pallas kernels  213 us (99%)
  local copies, waits for them, and re-layouts  2.34 us (1%)
    pallas_call x1, Pallas kernels, on_device(): pl.pallas_call(gather_factor, out_shape=[shape((2, BR, 2, 128, NB), BF),...  202 us
    pallas_call x1, Pallas kernels, on_device(): pl.pallas_call(update, grid=(BR,), out_shape=shape((BR, BC, NB, NB), BF),...  11.2 us

profile of v1, /device:TPU:144, one launch (start us, length us, event | category | flops | bytes accessed | tf_op | source)
XLA Modules:
  0.0 215.5 jit_solution(9766337156911917945)
XLA Ops:
  0.0 0.0 copy-start
  0.0 2.3 %copy-done = bf16[12,256,3,256]{3,1,2,0:T(8,128)(2,1)S(1)} copy-done((bf16[12,256,3,256]{3,1,2,0:T(8,128)(2,1)S(1)}, bf16[12,256,3,256]{3,1,2,0:T(8,128)(2,1)}, u32[]{:S(2)}) %copy-start) | copy-done | bytes 4718616
  2.3 201.9 %gather_factor.1 = (bf16[2,12,2,128,256]{4,3,2,1,0:T(8,128)(2,1)S(1)}, bf16[2,3,2,128,256]{4,3,2,1,0:T(8,128)(2,1)S(1)}, bf16[2,256,256]{2,1,0:T(8,128)(2,1)S(1)...) custom-call(bf16[12,3,2,128,256]{4,3,2,1,0:T(8,128)(2,1)S(1)} %bitcast.6), custom_call_target="tpu_custom_call" | custom-call | tf_op jit(solution)/shard_map/gather_factor/pallas_call | solution.py:417
  204.3 11.2 %update.1 = bf16[12,3,256,256]{3,2,1,0:T(8,128)(2,1)} custom-call(bf16[12,3,256,256]{3,2,1,0:T(8,128)(2,1)S(1)} %bitcast.7, bf16[2,12,256,256]{3,2,1,0:T(8,128)(2,1)S(1)} %bitcast.8, bf16[2,3,256,256]{3,2,1,0:T(8,128)(2,1)S(1)} %bitcast.9, bf16[2,256,256]{2,1,0:T(8,128)(2,1)S(1)} %get-tuple-element.14.packed, ...), custom_call_target="tpu_custom_call" | custom-call | tf_op jit(solution)/shard_map/update/pallas_call | solution.py:445
Async XLA Ops:
  0.0 2.3 %copy-start = (bf16[12,256,3,256]{3,1,2,0:T(8,128)(2,1)S(1)}, bf16[12,256,3,256]{3,1,2,0:T(8,128)(2,1)}, u32[]{:S(2)}) copy-start(bf16[12,256,3,256]{3,1,2,0:T(8,128)(2,1)} %param.1) | copy-start | bytes 14155780

commit v2 on v1

v2 whole, which is shorter than its diff:
```python
import functools

import jax
import jax.experimental.pallas as pl
import jax.experimental.pallas.tpu as pltpu
import jax.numpy as jnp
from jax import lax
from jax.sharding import PartitionSpec as P

NB = 256
B = 64
BR, BC = 12, 3
N_ROW, N_COL, N_Y, N_Z = 8, 32, 4, 8
F32, BF = jnp.float32, jnp.bfloat16
MESH = pl.DeviceIdType.MESH
HOP = 8
PRE1, PRE2 = 4, 16
TAIL = 3
assert all(PRE2 + 64 + TAIL * (i + 1) >= 6 * HOP + 5 * i + 4 for i in range(BR))


def recip(p):
    r = pl.reciprocal(p, approx=True)
    return r * (2.0 - p * r)

def bcast_lane(t, n):
    return jnp.broadcast_to(t[:, n:n + 1], (8, 128))

def bcast_row(t, j):
    return jnp.broadcast_to(t[j:j + 1, :], (8, 128))

def base(m1, m2, tick):
    sub = lax.broadcasted_iota(jnp.int32, (8, 128), 0)
    for k in range(8):
        tick(k)
        n = range(k, 8)
        v = {i: [bcast_lane(m1[i], 8 * k + j) for j in range(8)] for i in n}
        w = {i: [bcast_lane(m2[i], 8 * k + j) for j in range(8)] for i in n}
        scale = jnp.ones((8, 128), F32)
        for j in range(8):
            r = recip(bcast_row(v[k][j], j))
            scale = jnp.where(sub == j, r, scale)
            lv = {i: v[i][j] * r for i in n}
            lw = {i: w[i][j] * r for i in n}
            lv[k] = jnp.where(sub > j, lv[k], 0.0)
            lw[k] = jnp.where(sub > j, lw[k], 0.0)
            for t in range(j + 1, 8):
                a, b = bcast_row(v[k][t], j), bcast_row(w[k][t], j)
                for i in n:
                    v[i][t] = v[i][t] - lv[i] * a
                    w[i][t] = w[i][t] - lw[i] * b
            a, b = bcast_row(m1[k], j), bcast_row(m2[k], j)
            for i in n:
                m1[i] = m1[i] - lv[i] * a
                m2[i] = m2[i] - lw[i] * b
        m2[k] = m2[k] * scale
    return jnp.concatenate(m1, 0), jnp.concatenate(m2, 0)

def split(a):
    h = a.astype(BF)
    return h, (a - h.astype(F32)).astype(BF)

def dot3(a, b, nt=False):
    d = functools.partial(lax.dot_general, dimension_numbers=(((1,), (1 if nt else 0,)), ((), ())), preferred_element_type=F32)
    return d(a[0], b[0]) + (d(a[0], b[1]) + d(a[1], b[0]))

def factor(a1, a2, tick):
    eye = (lax.broadcasted_iota(jnp.int32, (B, B), 0) == lax.broadcasted_iota(jnp.int32, (B, B), 1)).astype(F32)
    for q in range(NB // B):
        s, e = q * B, (q + 1) * B
        d1 = jnp.concatenate([a1[s:e, s:e], eye], axis=1)
        d2 = jnp.concatenate([a2[s:e, s:e], eye], axis=1)
        m1, m2 = base(
            [d1[8 * i : 8 * i + 8] for i in range(8)], [d2[8 * i : 8 * i + 8] for i in range(8)],
            lambda k, q=q: tick(8 * q + k),
        )
        li, ui = split(m1[:, B:]), split(m2[:, B:])
        p1, p2 = dot3(li, split(a1[s:e, :])), dot3(ui, split(a2[s:e, :]))
        if e < NB:
            l21 = split(dot3(split(a1[e:, s:e]), ui, True))
            u12 = split(dot3(split(a2[e:, s:e]), li, True))
            a1[e:, :] = a1[e:, :] - dot3(l21, split(p1))
            a2[e:, :] = a2[e:, :] - dot3(u12, split(p2))
        a1[s:e, :] = p1
        a2[s:e, :] = p2
        a1[s:e, s:e] = m1[:, :B]
        a2[s:e, s:e] = m2[:, :B]


def load(a, a1, a2):
    ri = lax.broadcasted_iota(jnp.int32, (NB, NB), 0)
    ci = lax.broadcasted_iota(jnp.int32, (NB, NB), 1)
    eye = (ri == ci).astype(F32)
    for ref, x in ((a1, a), (a2, jnp.transpose(a))):
        ref[:, :NB] = x
        ref[:, NB:] = eye


def results(a1, a2):
    ri = lax.broadcasted_iota(jnp.int32, (NB, NB), 0)
    ci = lax.broadcasted_iota(jnp.int32, (NB, NB), 1)
    packed = jnp.where(ri <= ci, a1[:, :NB], jnp.transpose(a2[:, :NB]))
    return packed, a1[:, NB:], jnp.transpose(a2[:, NB:])


def nn(a, b):
    return jnp.dot(a, b, preferred_element_type=F32)


def gather_factor(
    a, mine, packed, linv, uinv, l10, u01, u, col, row, pieces, a1, a2,
    s1_send, s2_send, s3_send, p_recv, s3_recv,
    col_send, col_recv, row_send, row_recv, local_sem,
):
    r, c = lax.axis_index("row"), lax.axis_index("col")
    z, y = lax.div(c, N_Y), lax.rem(c, N_Y)
    core = lax.rem(r, 2)

    def send(src, dst, ssem, rsem, dev):
        return pltpu.make_async_remote_copy(
            src_ref=src, dst_ref=dst, send_sem=ssem, recv_sem=rsem, device_id=dev, device_id_type=MESH
        )

    barrier = pltpu.get_barrier_semaphore()

    @pl.loop(1, N_COL)
    def _(i):
        pl.semaphore_signal(barrier, inc=1, device_id=(r, lax.rem(c + i, N_COL)), device_id_type=MESH)

    @pl.loop(1, N_ROW)
    def _(i):
        pl.semaphore_signal(barrier, inc=1, device_id=(lax.rem(r + i, N_ROW), c), device_id_type=MESH)

    pl.semaphore_wait(barrier, N_COL - 1 + N_ROW - 1)

    def diag_piece(p):
        return a.at[0, 0, lax.div(p, 8), pl.ds(pl.multiple_of(lax.rem(lax.div(p, 2), 4) * 16, 16), 16),
                    pl.ds(pl.multiple_of(lax.rem(p, 2) * 128, 128), 128)]

    def own_copy(b):
        return pltpu.make_async_copy(diag_piece(c), pieces.at[b, c], p_recv.at[b])

    for b in range(4):
        @pl.when((r == b // 2) & (c == b % 2))
        def _(b=b):
            @pl.loop(1, N_COL)
            def _(i):
                dst = lax.rem(c + i, N_COL)
                send(diag_piece(dst), pieces.at[b, dst], s1_send.at[0], p_recv.at[b], (r, dst)).start()

            own_copy(b).start()

    dist_z = jnp.where(z == 0, 0, jnp.where(lax.rem(z, 4) == 2, 1, jnp.where(z == 4, 3, 2)))
    dist_y = [lax.rem(y - b + N_Y, N_Y) for b in range(2)]
    source = [(z == 0) & (dist_y[b] == 0) for b in range(2)]

    def load_panel(b):
        return pltpu.make_async_copy(a.at[:, 0], col.at[b], local_sem.at[0])

    def load_row():
        return pltpu.make_async_copy(a.at[0], row.at[core], local_sem.at[1])

    for b in range(2):
        @pl.when(source[b])
        def _(b=b):
            load_panel(b).start()

    @pl.when(r < 2)
    def _():
        load_row().start()

    load_mine = pltpu.make_async_copy(a, mine, local_sem.at[2])
    load_mine.start()

    def arrived(b):
        own = (r == b // 2) & (c == b % 2)

        @pl.when(own)
        def _():
            own_copy(b).wait()

        @pl.when(jnp.logical_not(own))
        def _():
            send(pieces.at[b, c], pieces.at[b, c], s1_send.at[0], p_recv.at[b], (r, c)).wait_recv()

    def to_rows(b):
        for i in range(1, N_ROW):
            dst = lax.rem(r + i, N_ROW)
            yield send(pieces.at[b, c], pieces.at[b, c], s2_send.at[b % 2, i - 1], p_recv.at[b], (dst, c))

    def spread_rows(blocks):
        for b in blocks:
            @pl.when(r == b // 2)
            def _(b=b):
                arrived(b)
                for copy in to_rows(b):
                    copy.start()

    def to_cols(kind, dst):
        block = pieces.at[pl.ds(kind, 1 + 2 * kind), c]
        return send(block, block, s3_send.at[kind], s3_recv.at[kind], (r, dst))

    def spread_cols(kind, blocks):
        for b in blocks:
            @pl.when(r != b // 2)
            def _(b=b):
                arrived(b)

        @pl.loop(1, N_COL)
        def _(i):
            to_cols(kind, lax.rem(c + i, N_COL)).start()

    def all_pieces(kind):
        block = pieces.at[pl.ds(kind, 1 + 2 * kind), pl.ds(0, N_COL - 1)]
        return send(block, block, s3_send.at[kind], s3_recv.at[kind], (r, c))

    def forwards(b, half):
        z_one = (dist_y[b] == 0) & ((z == 0) | (z == 2) | (z == 3) | (z == 6))
        z_two = (dist_y[b] == 0) & ((z == 0) | (z == 2) | (z == 6))
        z_one_dst = jnp.where(z == 0, 2, jnp.where(z == 6, 5, lax.rem(z + 1, N_Z))) * N_Y + y
        z_two_dst = jnp.where(z == 0, 6, jnp.where(z == 2, 1, 7)) * N_Y + y
        if half == 0:
            y_on, y_dst = dist_y[b] <= 2, lax.rem(y + 1, N_Y)
        else:
            y_on, y_dst = dist_y[b] != 1, lax.rem(y + N_Y - 1, N_Y)
        return ((z_one, z_one_dst), (z_two, z_two_dst), (y_on, z * N_Y + y_dst))

    def chunk_copy(b, half, sub, i, way, dst, first=False):
        k = 2 * half + sub
        block = col.at[b, i, k]
        return send(a.at[i, 0, k] if first else block, block, col_send.at[b, k, i, way], col_recv.at[b, k, i], (r, dst))

    def relay(slot):
        for b in range(2):
            for half in range(2):
                dist = dist_z + (dist_y[b] if half == 0 else lax.rem(N_Y - dist_y[b], N_Y))
                m = slot - HOP * dist
                i = lax.div(m, 5)
                rest = lax.rem(m, 5) - half
                sub = lax.div(rest, 2)

                @pl.when((m >= 0) & ((rest == 0) | (rest == 2)) & (i < BR))
                def _(b=b, half=half, i=i, sub=sub):
                    @pl.when(jnp.logical_not(source[b]))
                    def _():
                        chunk_copy(b, half, sub, i, 0, c).wait_recv()
                        forward(b, half, sub, i)

                    @pl.when(source[b])
                    def _():
                        forward(b, half, sub, i, True)

    def forward(b, half, sub, i, first=False):
        for way, (on, dst) in enumerate(forwards(b, half)):
            @pl.when(on)
            def _(way=way, dst=dst):
                chunk_copy(b, half, sub, i, way, dst, first).start()

    def row_copy(i, dst):
        block = row.at[core]
        return send(block, block, row_send.at[i], row_recv.at[core], (dst, c))

    def row_out_start():
        @pl.when(r < 2)
        def _():
            for i in range(1, 4):
                row_copy(i, r + 2 * i).start()

    def row_swap():
        @pl.when(r >= 2)
        def _():
            row_copy(0, r).wait_recv()

        row_copy(0, r + 1 - 2 * core).start()

    spread_rows((0,))

    @pl.loop(0, PRE1)
    def _(slot):
        relay(slot)

    spread_cols(0, (0,))

    @pl.loop(PRE1, PRE2)
    def _(slot):
        relay(slot)

    @pl.when(r < 2)
    def _():
        load_row().wait()

    all_pieces(0).wait_recv()

    def whole(b):
        x = pieces[b].astype(F32).reshape(16, 2, 16, 128)
        return jnp.concatenate([x[:, 0].reshape(NB, 128), x[:, 1].reshape(NB, 128)], 1)

    load(whole(0), a1, a2)

    @pl.loop(0, 2)
    def _(step):
        @pl.when(step == 1)
        def _():
            all_pieces(1).wait_recv()
            l10[...] = nn(whole(2).astype(BF), uinv[0]).astype(BF)
            u01[...] = nn(linv[0], whole(1).astype(BF)).astype(BF)
            load((whole(3) - nn(l10[...], u01[...])).astype(BF).astype(F32), a1, a2)

        def tick(k):
            relay(PRE2 + step * 32 + k)
            if k == 1:
                @pl.when(step == 0)
                def _():
                    spread_rows((1, 2, 3))

            if k == 3:
                @pl.when(step == 0)
                def _():
                    spread_cols(1, (1, 2, 3))

            if k == 5:
                @pl.when(step == 0)
                def _():
                    row_out_start()

            if k == 13:
                @pl.when(step == 1)
                def _():
                    row_swap()

        factor(a1, a2, tick)
        pk, li, ui = results(a1, a2)
        packed[step] = pk.astype(BF)
        linv[step] = li.astype(BF)
        uinv[step] = ui.astype(BF)

    for b in range(2):
        @pl.when(source[b])
        def _(b=b):
            load_panel(b).wait()

    load_mine.wait()
    other = row.at[1 - core]
    send(other, other, row_send.at[0], row_recv.at[1 - core], (r, c)).wait_recv()
    for j in range(BC):
        h = j * N_COL + c
        u0 = jnp.where(h > 0, nn(linv[0], row[0, j].reshape(NB, NB)), 0.0).astype(BF)
        row1 = (row[1, j].reshape(NB, NB).astype(F32) - nn(l10[...], u0)).astype(BF)
        u[0, j] = u0
        u[1, j] = jnp.where(h > 1, nn(linv[1], row1), 0.0).astype(BF)

    @pl.loop(0, BR)
    def _(i):
        for k in range(TAIL):
            relay(PRE2 + 64 + TAIL * i + k)
        update(i, r, c, mine, col, packed, uinv, u01, u)

    for b in range(4):
        @pl.when((r == b // 2) & (c == b % 2))
        def _(b=b):
            block = pieces.at[0, pl.ds(0, N_COL - 1)]
            send(block, block, s1_send.at[0], p_recv.at[b], (r, c)).wait_send()

        @pl.when(r == b // 2)
        def _(b=b):
            for copy in to_rows(b):
                copy.wait_send()

    for kind in range(2):
        all_pieces(kind).wait_send()

    @pl.when(r < 2)
    def _():
        for i in range(1, 4):
            row_copy(i, r).wait_send()

    row_copy(0, r).wait_send()

    for b in range(2):
        for half in range(2):
            for way, (on, dst) in enumerate(forwards(b, half)):
                @pl.when(on)
                def _(b=b, half=half, way=way, dst=dst):
                    @pl.loop(0, BR)
                    def _(i):
                        for sub in range(2):
                            chunk_copy(b, half, sub, i, way, dst).wait_send()


def update(i, r, c, mine, col, packed, uinv, u01, u):
    g = i * N_ROW + r
    l0 = jnp.where(g > 0, nn(col[0, i].reshape(NB, NB), uinv[0]), 0.0).astype(BF)
    c1 = (col[1, i].reshape(NB, NB).astype(F32) - nn(l0, u01[...])).astype(BF)
    l1 = jnp.where(g > 1, nn(c1, uinv[1]), 0.0).astype(BF)

    def put(j, x):
        mine[i, j] = x.reshape(4, 64, NB)

    for j in range(BC):
        x = (mine[i, j].reshape(NB, NB).astype(F32) - nn(l0, u[0, j])).astype(BF)
        put(j, (x.astype(F32) - nn(l1, u[1, j])).astype(BF))

    @pl.when(c == 0)
    def _():
        put(0, jnp.where(g > 0, l0, packed[0]))

    @pl.when((c == 1) & (g > 0))
    def _():
        put(0, jnp.where(g > 1, l1, packed[1]))

    for k in range(2):
        @pl.when(g == k)
        def _(k=k):
            for j in range(BC):
                @pl.when(j * N_COL + c > k)
                def _(j=j):
                    put(j, u[k, j])


def on_device(matrix):
    dma = pltpu.SemaphoreType.DMA
    hbm = pl.BlockSpec(memory_space=pl.ANY)
    out = pl.pallas_call(
        gather_factor,
        out_shape=pltpu.VMEM((BR, BC, 4, 64, NB), BF),
        in_specs=[hbm],
        out_specs=pl.BlockSpec(memory_space=pltpu.VMEM),
        scratch_shapes=[
            pltpu.VMEM((2, NB, NB), BF),
            pltpu.VMEM((2, NB, NB), BF),
            pltpu.VMEM((2, NB, NB), BF),
            pltpu.VMEM((NB, NB), BF),
            pltpu.VMEM((NB, NB), BF),
            pltpu.VMEM((2, BC, NB, NB), BF),
            pltpu.VMEM((2, BR, 4, 64, NB), BF),
            pltpu.VMEM((2, BC, 4, 64, NB), BF),
            pltpu.VMEM((4, N_COL, 16, 128), BF),
            pltpu.VMEM((NB, 2 * NB), F32),
            pltpu.VMEM((NB, 2 * NB), F32),
            dma((1,)), dma((2, N_ROW - 1)), dma((2,)), dma((4,)), dma((2,)),
            dma((2, 4, BR, 3)), dma((2, 4, BR)), dma((4,)), dma((2,)), dma((3,)),
        ],
        compiler_params=pltpu.CompilerParams(
            collective_id=0, has_side_effects=True, vmem_limit_bytes=58 << 20
        ),
        name="gather_factor",
    )(matrix.transpose(0, 2, 1, 3).reshape(BR, BC, 4, 64, NB))
    return out.reshape(BR, BC, NB, NB).transpose(0, 2, 1, 3)


def solution(mesh):
    placed = (P(None, "row", None, "col"),)
    return jax.shard_map(
        on_device,
        mesh=mesh,
        in_specs=placed,
        out_specs=P(None, "row", None, "col"),
        check_vma=False,
    )
```

time: 216 us -> 90.9 us (0.42)
  the two profiles are of different devices: /device:TPU:144 before, /device:TPU:36 now
where the time goes in v2:
time: 90.9 us; the launch traced here: 90.8 us
  Pallas kernels  88.6 us (97%)
  local copies, waits for them, and re-layouts  2.19 us (2%)
    pallas_call x1, Pallas kernels, on_device(): pl.pallas_call(gather_factor, out_shape=pltpu.VMEM((BR, BC, 4, 64, NB), B...  88.6 us
    unnamed x1, local copies, waits for them, and re-layouts  2.19 us

profile of v2, /device:TPU:36, one launch (start us, length us, event | category | flops | bytes accessed | tf_op | source)
XLA Modules:
  0.0 90.8 jit_solution(3844138321382557711)
XLA Ops:
  0.0 88.6 %gather_factor.1 = bf16[12,3,4,64,256]{4,3,2,1,0:T(8,128)(2,1)S(1)} custom-call(bf16[12,3,4,64,256]{4,3,2,1,0:T(8,128)(2,1)} %bitcast.7), custom_call_target="tpu_custom_call" | custom-call | tf_op jit(solution)/shard_map/gather_factor/pallas_call | solution.py:423
  88.6 2.2 %copy.3 = bf16[12,256,3,256]{3,1,2,0:T(8,128)(2,1)} copy(bf16[12,256,3,256]{3,1,2,0:T(8,128)(2,1)S(1)} %bitcast.6) | data formatting | bytes 9437184

commit v3 on v2

--- a/solution.py
+++ b/solution.py
@@ -13,10 +13,13 @@
 N_ROW, N_COL, N_Y, N_Z = 8, 32, 4, 8
 F32, BF = jnp.float32, jnp.bfloat16
 MESH = pl.DeviceIdType.MESH
-HOP = 8
-PRE1, PRE2 = 4, 16
-TAIL = 3
-assert all(PRE2 + 64 + TAIL * (i + 1) >= 6 * HOP + 5 * i + 4 for i in range(BR))
+UNITS = 8
+HOP = 2
+LATE = 3
+PRE1, PRE2 = 2, 6
+GROUP = 3
+TAIL = 1
+assert all(PRE2 + 2 * UNITS + TAIL * (i + 1) >= 6 * HOP + GROUP * (i + 1) for i in range(BR // GROUP))
 
 
 def recip(p):
@@ -134,7 +137,7 @@
     pl.semaphore_wait(barrier, N_COL - 1 + N_ROW - 1)
 
     def diag_piece(p):
-        return a.at[0, 0, lax.div(p, 8), pl.ds(pl.multiple_of(lax.rem(lax.div(p, 2), 4) * 16, 16), 16),
+        return a.at[0, 0, lax.div(p, 16), pl.ds(pl.multiple_of(lax.rem(lax.div(p, 2), 8) * 16, 16), 16),
                     pl.ds(pl.multiple_of(lax.rem(p, 2) * 128, 128), 128)]
 
     def own_copy(b):
@@ -214,47 +217,64 @@
         block = pieces.at[pl.ds(kind, 1 + 2 * kind), pl.ds(0, N_COL - 1)]
         return send(block, block, s3_send.at[kind], s3_recv.at[kind], (r, c))
 
-    def forwards(b, half):
-        z_one = (dist_y[b] == 0) & ((z == 0) | (z == 2) | (z == 3) | (z == 6))
-        z_two = (dist_y[b] == 0) & ((z == 0) | (z == 2) | (z == 6))
+    lanes = [[0, 3], [1, 2]]
+
+    def from_lane(b, half):
+        return lax.rem(y - lanes[b][half] + N_Y, N_Y)
+
+    def ring(d):
+        return jnp.minimum(d, N_Y - d)
+
+    def distance(b, half):
+        first = ring(dist_y[b]) + (LATE * jnp.minimum(dist_y[b], 1) if half == 0 else 0)
+        return jnp.where(z == 0, first, dist_z + half + ring(from_lane(b, half)))
+
+    def along_z(b, half, i):
+        on = from_lane(b, half) == 0
+        z_one = on & ((z == 0) | (z == 2) | (z == 3) | (z == 6))
+        z_two = on & ((z == 0) | (z == 2) | (z == 6))
         z_one_dst = jnp.where(z == 0, 2, jnp.where(z == 6, 5, lax.rem(z + 1, N_Z))) * N_Y + y
         z_two_dst = jnp.where(z == 0, 6, jnp.where(z == 2, 1, 7)) * N_Y + y
-        if half == 0:
-            y_on, y_dst = dist_y[b] <= 2, lax.rem(y + 1, N_Y)
-        else:
-            y_on, y_dst = dist_y[b] != 1, lax.rem(y + N_Y - 1, N_Y)
-        return ((z_one, z_one_dst), (z_two, z_two_dst), (y_on, z * N_Y + y_dst))
-
-    def chunk_copy(b, half, sub, i, way, dst, first=False):
-        k = 2 * half + sub
-        block = col.at[b, i, k]
-        return send(a.at[i, 0, k] if first else block, block, col_send.at[b, k, i, way], col_recv.at[b, k, i], (r, dst))
-
-    def relay(slot):
+        return ((0, z_one, z_one_dst), (1, z_two, z_two_dst))
+
+    def along_y(b, half, i):
+        d, e, odd = from_lane(b, half), dist_y[b], lax.rem(i, 2)
+        here = (z == 0) & ((e == 0) | (e == (3, 1)[b]))
+        up = (e == 0) if b == 0 else here
+        down = here if b == 0 else (e == 0)
+        up = ((z == 0) & up) | ((z > 0) & ((d == 0) | ((d == 1) & (odd == 0))))
+        down = ((z == 0) & down) | ((z > 0) & ((d == 0) | ((d == 3) & (odd == 1))))
+        return ((2, up, z * N_Y + lax.rem(y + 1, N_Y)), (3, down, z * N_Y + lax.rem(y + N_Y - 1, N_Y)))
+
+    def chunk_copy(b, half, i, way, dst, first=False):
+        block = col.at[b, i, half]
+        return send(a.at[i, 0, half] if first else block, block, col_send.at[b, half, i, way],
+                    col_recv.at[b, half, i], (r, dst))
+
+    def relay(unit, half):
         for b in range(2):
-            for half in range(2):
-                dist = dist_z + (dist_y[b] if half == 0 else lax.rem(N_Y - dist_y[b], N_Y))
-                m = slot - HOP * dist
-                i = lax.div(m, 5)
-                rest = lax.rem(m, 5) - half
-                sub = lax.div(rest, 2)
-
-                @pl.when((m >= 0) & ((rest == 0) | (rest == 2)) & (i < BR))
-                def _(b=b, half=half, i=i, sub=sub):
-                    @pl.when(jnp.logical_not(source[b]))
-                    def _():
-                        chunk_copy(b, half, sub, i, 0, c).wait_recv()
-                        forward(b, half, sub, i)
-
-                    @pl.when(source[b])
-                    def _():
-                        forward(b, half, sub, i, True)
-
-    def forward(b, half, sub, i, first=False):
-        for way, (on, dst) in enumerate(forwards(b, half)):
-            @pl.when(on)
-            def _(way=way, dst=dst):
-                chunk_copy(b, half, sub, i, way, dst, first).start()
+            i = unit - HOP * distance(b, half)
+
+            @pl.when(jnp.logical_not(source[b]) & (i >= 0) & (i < BR))
+            def _(b=b, i=i):
+                chunk_copy(b, half, i, 0, c).wait_recv()
+                forward(b, half, i, (along_z, along_y))
+
+            @pl.when(source[b])
+            def _(b=b):
+                for ways, late in ((along_z, 0), (along_y, HOP * LATE if half == 0 else 0)):
+                    i = unit - late
+
+                    @pl.when((i >= 0) & (i < BR))
+                    def _(ways=ways, i=i):
+                        forward(b, half, i, (ways,), True)
+
+    def forward(b, half, i, kinds, first=False):
+        for kind in kinds:
+            for way, on, dst in kind(b, half, i):
+                @pl.when(on)
+                def _(way=way, dst=dst):
+                    chunk_copy(b, half, i, way, dst, first).start()
 
     def row_copy(i, dst):
         block = row.at[core]
@@ -273,17 +293,19 @@
 
         row_copy(0, r + 1 - 2 * core).start()
 
+    @pl.loop(0, PRE1)
+    def _(unit):
+        relay(unit, 1)
+        relay(unit, 0)
+
     spread_rows((0,))
 
-    @pl.loop(0, PRE1)
-    def _(slot):
-        relay(slot)
-
     spread_cols(0, (0,))
 
     @pl.loop(PRE1, PRE2)
-    def _(slot):
-        relay(slot)
+    def _(unit):
+        relay(unit, 1)
+        relay(unit, 0)
 
     @pl.when(r < 2)
     def _():
@@ -296,6 +318,8 @@
         return jnp.concatenate([x[:, 0].reshape(NB, 128), x[:, 1].reshape(NB, 128)], 1)
 
     load(whole(0), a1, a2)
+
+    halves = [[(32 * i + 16 * (1 - half)) // UNITS for i in range(UNITS)] for half in range(2)]
 
     @pl.loop(0, 2)
     def _(step):
@@ -307,7 +331,10 @@
             load((whole(3) - nn(l10[...], u01[...])).astype(BF).astype(F32), a1, a2)
 
         def tick(k):
-            relay(PRE2 + step * 32 + k)
+            for half in (1, 0):
+                if k in halves[half]:
+                    relay(PRE2 + step * UNITS + halves[half].index(k), half)
+
             if k == 1:
                 @pl.when(step == 0)
                 def _():
@@ -349,10 +376,12 @@
         u[0, j] = u0
         u[1, j] = jnp.where(h > 1, nn(linv[1], row1), 0.0).astype(BF)
 
-    @pl.loop(0, BR)
+    @pl.loop(0, BR // GROUP)
     def _(i):
         for k in range(TAIL):
-            relay(PRE2 + 64 + TAIL * i + k)
+            for half in (1, 0):
+                relay(PRE2 + 2 * UNITS + TAIL * i + k, half)
+
         update(i, r, c, mine, col, packed, uinv, u01, u)
 
     for b in range(4):
@@ -378,43 +407,46 @@
 
     for b in range(2):
         for half in range(2):
-            for way, (on, dst) in enumerate(forwards(b, half)):
-                @pl.when(on)
-                def _(b=b, half=half, way=way, dst=dst):
-                    @pl.loop(0, BR)
-                    def _(i):
-                        for sub in range(2):
-                            chunk_copy(b, half, sub, i, way, dst).wait_send()
+            @pl.loop(0, BR)
+            def _(i, b=b, half=half):
+                for way, on, dst in along_z(b, half, i) + along_y(b, half, i):
+                    @pl.when(on)
+                    def _(way=way, dst=dst):
+                        chunk_copy(b, half, i, way, dst).wait_send()
 
 
 def update(i, r, c, mine, col, packed, uinv, u01, u):
-    g = i * N_ROW + r
-    l0 = jnp.where(g > 0, nn(col[0, i].reshape(NB, NB), uinv[0]), 0.0).astype(BF)
-    c1 = (col[1, i].reshape(NB, NB).astype(F32) - nn(l0, u01[...])).astype(BF)
-    l1 = jnp.where(g > 1, nn(c1, uinv[1]), 0.0).astype(BF)
-
-    def put(j, x):
-        mine[i, j] = x.reshape(4, 64, NB)
-
+    rows = pl.ds(pl.multiple_of(i * GROUP, GROUP), GROUP)
+    high = GROUP * NB
+    later = (lax.broadcasted_iota(jnp.int32, (high, NB), 0) >= NB) | (i > 0)
+    l0 = jnp.where(later | (r > 0), nn(col[0, rows].reshape(high, NB), uinv[0]), 0.0).astype(BF)
+    c1 = (col[1, rows].reshape(high, NB).astype(F32) - nn(l0, u01[...])).astype(BF)
+    l1 = jnp.where(later | (r > 1), nn(c1, uinv[1]), 0.0).astype(BF)
     for j in range(BC):
-        x = (mine[i, j].reshape(NB, NB).astype(F32) - nn(l0, u[0, j])).astype(BF)
-        put(j, (x.astype(F32) - nn(l1, u[1, j])).astype(BF))
+        x = (mine[rows, j].reshape(high, NB).astype(F32) - nn(l0, u[0, j])).astype(BF)
+        x = (x.astype(F32) - nn(l1, u[1, j])).astype(BF)
+        mine[rows, j] = x.reshape(GROUP, 2, 128, NB)
 
     @pl.when(c == 0)
     def _():
-        put(0, jnp.where(g > 0, l0, packed[0]))
-
-    @pl.when((c == 1) & (g > 0))
+        mine[rows, 0] = l0.reshape(GROUP, 2, 128, NB)
+
+    @pl.when(c == 1)
     def _():
-        put(0, jnp.where(g > 1, l1, packed[1]))
+        kept = mine[rows, 0].reshape(high, NB)
+        mine[rows, 0] = jnp.where(later | (r > 1), l1, kept).reshape(GROUP, 2, 128, NB)
 
     for k in range(2):
-        @pl.when(g == k)
+        @pl.when((i == 0) & (r == k))
         def _(k=k):
             for j in range(BC):
                 @pl.when(j * N_COL + c > k)
                 def _(j=j):
-                    put(j, u[k, j])
+                    mine[0, j] = u[k, j].reshape(2, 128, NB)
+
+            @pl.when(c == k)
+            def _():
+                mine[0, 0] = packed[k].reshape(2, 128, NB)
 
 
 def on_device(matrix):
@@ -422,7 +454,7 @@
     hbm = pl.BlockSpec(memory_space=pl.ANY)
     out = pl.pallas_call(
         gather_factor,
-        out_shape=pltpu.VMEM((BR, BC, 4, 64, NB), BF),
+        out_shape=pltpu.VMEM((BR, BC, 2, 128, NB), BF),
         in_specs=[hbm],
         out_specs=pl.BlockSpec(memory_space=pltpu.VMEM),
         scratch_shapes=[
@@ -432,19 +464,19 @@
             pltpu.VMEM((NB, NB), BF),
             pltpu.VMEM((NB, NB), BF),
             pltpu.VMEM((2, BC, NB, NB), BF),
-            pltpu.VMEM((2, BR, 4, 64, NB), BF),
-            pltpu.VMEM((2, BC, 4, 64, NB), BF),
+            pltpu.VMEM((2, BR, 2, 128, NB), BF),
+            pltpu.VMEM((2, BC, 2, 128, NB), BF),
             pltpu.VMEM((4, N_COL, 16, 128), BF),
             pltpu.VMEM((NB, 2 * NB), F32),
             pltpu.VMEM((NB, 2 * NB), F32),
             dma((1,)), dma((2, N_ROW - 1)), dma((2,)), dma((4,)), dma((2,)),
-            dma((2, 4, BR, 3)), dma((2, 4, BR)), dma((4,)), dma((2,)), dma((3,)),
+            dma((2, 2, BR, 4)), dma((2, 2, BR)), dma((4,)), dma((2,)), dma((3,)),
         ],
         compiler_params=pltpu.CompilerParams(
             collective_id=0, has_side_effects=True, vmem_limit_bytes=58 << 20
         ),
         name="gather_factor",
-    )(matrix.transpose(0, 2, 1, 3).reshape(BR, BC, 4, 64, NB))
+    )(matrix.transpose(0, 2, 1, 3).reshape(BR, BC, 2, 128, NB))
     return out.reshape(BR, BC, NB, NB).transpose(0, 2, 1, 3)
 
 

time: 90.9 us -> 80.2 us (0.88)
  Pallas kernels: 88.6 us -> 77.9 us
    pallas_call x1, Pallas kernels: 88.6 us -> 77.9 us  [on_device(): pl.pallas_call(gather_factor, out_shape=pltpu.VMEM((BR, BC, 2, 128, NB),...]
where the time goes in v3:
time: 80.2 us; the launch traced here: 80.1 us
  Pallas kernels  77.9 us (97%)
  local copies, waits for them, and re-layouts  2.19 us (3%)
    pallas_call x1, Pallas kernels, on_device(): pl.pallas_call(gather_factor, out_shape=pltpu.VMEM((BR, BC, 2, 128, NB),...  77.9 us
    unnamed x1, local copies, waits for them, and re-layouts  2.19 us

profile of v3, /device:TPU:36, one launch (start us, length us, event | category | flops | bytes accessed | tf_op | source)
XLA Modules:
  0.0 80.1 jit_solution(2892674558485565787)
XLA Ops:
  0.0 77.9 %gather_factor.1 = bf16[12,3,2,128,256]{4,3,2,1,0:T(8,128)(2,1)S(1)} custom-call(bf16[12,3,2,128,256]{4,3,2,1,0:T(8,128)(2,1)} %bitcast.7), custom_call_target="tpu_custom_call" | custom-call | tf_op jit(solution)/shard_map/gather_factor/pallas_call | solution.py:455
  77.9 2.2 %copy.3 = bf16[12,256,3,256]{3,1,2,0:T(8,128)(2,1)} copy(bf16[12,256,3,256]{3,1,2,0:T(8,128)(2,1)S(1)} %bitcast.6) | data formatting | bytes 9437184

commit v4 on v3

--- a/solution.py
+++ b/solution.py
@@ -13,10 +13,10 @@
 N_ROW, N_COL, N_Y, N_Z = 8, 32, 4, 8
 F32, BF = jnp.float32, jnp.bfloat16
 MESH = pl.DeviceIdType.MESH
-UNITS = 8
+UNITS = 7
 HOP = 2
 LATE = 3
-PRE1, PRE2 = 2, 6
+PRE1, PRE2 = 3, 8
 GROUP = 3
 TAIL = 1
 assert all(PRE2 + 2 * UNITS + TAIL * (i + 1) >= 6 * HOP + GROUP * (i + 1) for i in range(BR // GROUP))

time: 80.2 us -> 79.1 us (0.986)
  Pallas kernels: 77.9 us -> 76.8 us
    pallas_call x1, Pallas kernels: 77.9 us -> 76.8 us  [on_device(): pl.pallas_call(gather_factor, out_shape=pltpu.VMEM((BR, BC, 2, 128, NB),...]
where the time goes in v4:
time: 79.1 us; the launch traced here: 79 us
  Pallas kernels  76.8 us (97%)
  local copies, waits for them, and re-layouts  2.19 us (3%)
    pallas_call x1, Pallas kernels, on_device(): pl.pallas_call(gather_factor, out_shape=pltpu.VMEM((BR, BC, 2, 128, NB),...  76.8 us
    unnamed x1, local copies, waits for them, and re-layouts  2.19 us

profile of v4, /device:TPU:36, one launch (start us, length us, event | category | flops | bytes accessed | tf_op | source)
XLA Modules:
  0.0 79.0 jit_solution(5839097006536756880)
XLA Ops:
  0.0 76.8 %gather_factor.1 = bf16[12,3,2,128,256]{4,3,2,1,0:T(8,128)(2,1)S(1)} custom-call(bf16[12,3,2,128,256]{4,3,2,1,0:T(8,128)(2,1)} %bitcast.7), custom_call_target="tpu_custom_call" | custom-call | tf_op jit(solution)/shard_map/gather_factor/pallas_call | solution.py:455
  76.8 2.2 %copy.3 = bf16[12,256,3,256]{3,1,2,0:T(8,128)(2,1)} copy(bf16[12,256,3,256]{3,1,2,0:T(8,128)(2,1)S(1)} %bitcast.6) | data formatting | bytes 9437184
